TPU v7x, 512 devices: a whole 4x8x8 slice. The times are simulated.
512 devices in a mesh: rep: 32 (over x, z), fsdp: 16 (over y, core).
Axes of the slice: x: 4, y: 8, z: 8, core: 2. Of those that a mesh axis runs over, the one named last changes fastest.
Arguments:
- deltas: bfloat16 [32, 2, 4096, 512], P('rep', None, 'fsdp'), may hold values from -64 to 64
- weights: float32 [2, 4096, 512], P(None, 'fsdp'), may hold values from -6 to 6
- momentum: float32 [2, 4096, 512], P(None, 'fsdp'), may hold values from -0.6 to 0.6
- warm_factors: float32 [512, 2, 256], P('fsdp'), may hold values from -6 to 6
- matrix_ranks: int32 [2], replicated, may hold values from 32 to 256
Outputs:
- new_weights: float32 [2, 4096, 512], P(None, 'fsdp')
- new_momentum: float32 [2, 4096, 512], P(None, 'fsdp')
- new_factors: float32 [512, 2, 256], P('fsdp')
All inputs are finite; a program needn't handle non-finite values.
Results may differ from a plain program's by a relative error of at most 0.0057.
Values may be sent and summed in bfloat16 or wider, within the bound.
A program may use at most 64 MiB of HBM per device.

v0:
```python
import jax
import jax.numpy as jnp
from jax import lax
from jax.sharding import PartitionSpec as P

OUTER_RATE = 0.7
OUTER_MOMENTUM = 0.9


def column_mask(matrix_ranks, rank_width):
    columns = jnp.arange(rank_width, dtype=jnp.int32)
    return (columns[None, :] < matrix_ranks[:, None]).astype(jnp.float32)


def gram_of(factor):
    return jnp.einsum("mrk,mrj->mkj", factor, factor, precision=lax.Precision.HIGHEST)


def orthonormal_of(gram_matrix, factor):
    chol_factor = jnp.linalg.cholesky(gram_matrix)
    solved = lax.linalg.triangular_solve(
        chol_factor, factor, left_side=False, lower=True, transpose_a=True
    )
    return solved.astype(jnp.bfloat16)


def shards(deltas, weights, momentum, warm_factors, matrix_ranks):
    rank_width = warm_factors.shape[2]
    replicas = lax.axis_size("rep")
    rank_mask = column_mask(matrix_ranks, rank_width)
    filler = jnp.eye(rank_width, dtype=jnp.float32)[None] * (1.0 - rank_mask)[:, None, :]
    own_delta = deltas[0]
    warm = warm_factors.astype(jnp.bfloat16) * rank_mask[None].astype(jnp.bfloat16)
    warm_full = lax.all_gather(warm, "fsdp", axis=0, tiled=True)
    partial_left = jnp.einsum(
        "mrc,cmk->mrk", own_delta, warm_full, preferred_element_type=jnp.float32
    )
    left_factor = lax.psum(partial_left, "rep") / replicas
    gram_matrix = lax.psum(gram_of(left_factor), "fsdp") + filler
    orthonormal = orthonormal_of(gram_matrix, left_factor)
    column_share = lax.psum_scatter(
        jnp.einsum("mrc,mrk->cmk", own_delta, orthonormal, preferred_element_type=jnp.float32),
        "fsdp",
        scatter_dimension=0,
        tiled=True,
    )
    new_factors = lax.psum(column_share, "rep") / replicas
    factors_full = lax.all_gather(new_factors.astype(jnp.bfloat16), "fsdp", axis=0, tiled=True)
    approx = jnp.einsum(
        "mrk,cmk->mrc", orthonormal, factors_full, preferred_element_type=jnp.float32
    )
    new_momentum = OUTER_MOMENTUM * momentum + approx
    new_weights = weights - OUTER_RATE * (approx + OUTER_MOMENTUM * new_momentum)
    return (new_weights, new_momentum, new_factors)


def solution(mesh):
    placed = (
        P("rep", None, "fsdp", None),
        P(None, "fsdp", None),
        P(None, "fsdp", None),
        P("fsdp", None, None),
        P(),
    )
    return jax.shard_map(
        shards,
        mesh=mesh,
        in_specs=placed,
        out_specs=(P(None, "fsdp", None), P(None, "fsdp", None), P("fsdp", None, None)),
        check_vma=False,
    )
```

profile of v0, /device:TPU:1, one launch (start us, length us, event | category | flops | bytes accessed | tf_op | source)
XLA Modules:
  0.0 726.0 jit_solution(954331956540465368)
XLA Ops:
  7.2 0.8 fusion.14
  8.0 0.8 fusion.12
  8.8 22.4 %all_gather.6 = bf16[512,2,256]{2,0,1:T(8,128)(2,1)S(1)} all-gather(bf16[32,2,256]{2,0,1:T(8,128)(2,1)S(1)} %fusion.12), channel_id=1, replica_groups=mesh['rep'=32,'fsdp'=16] {'fsdp'}, dimensions={0}, use_global_device_ids=true | all-gather | bytes 557056 | tf_op jit(solution)/shard_map/all_gather | solution.py:34
  31.3 1.1 convolution_bitcast_fusion.1
  32.6 0.6 copy-done.5
  33.3 153.2 %all-reduce.7.cloned.1.call-done = f32[2,256,256]{1,2,0:T(8,128)} async-done(((f32[2,256,256]{1,2,0:T(8,128)}), f32[2,256,256]{1,2,0:T(8,128)}) %all-reduce.7.cloned.1.call-update) | async-done | bytes 524304 | tf_op jit(solution)/shard_map/psum | solution.py:38
  186.5 2.7 fusion.17
  189.3 0.9 copy-done.1
  190.3 115.0 %all-reduce.9.cloned.1.call-done = f32[2,256,256]{1,2,0:T(8,128)} async-done(((f32[2,256,256]{1,2,0:T(8,128)}), f32[2,256,256]{1,2,0:T(8,128)}) %all-reduce.9.cloned.1.call-update) | async-done | bytes 524304 | tf_op jit(solution)/shard_map/psum | solution.py:39
  305.2 1.2 multiply_add_fusion.1
  306.6 0.8 copy-done.2
  307.6 23.5 %custom-call.16 = f32[2,128,128]{2,1,0:T(8,128)S(1)} custom-call(f32[2,128,128]{2,1,0:T(8,128)S(1)} %cholesky.122), custom_call_target="Cholesky" | custom-call | tf_op jit(solution)/shard_map/jit(cholesky)/cholesky | solution.py:20
  331.1 19.7 %custom-call.17 = f32[2,1,128,128]{2,3,1,0:T(8,128)S(1)} custom-call(f32[2,1,128,128]{3,2,1,0:T(8,128)S(1)} %select_bitcast_fusion), custom_call_target="InvertDiagBlocksLowerTriangular" | custom-call | tf_op jit(solution)/shard_map/jit(cholesky)/cholesky | solution.py:20
  351.1 0.4 convolution_subtract_fusion.1
  351.5 23.5 %custom-call.18 = f32[2,128,128]{2,1,0:T(8,128)S(1)} custom-call(f32[2,128,128]{2,1,0:T(8,128)S(1)} %convolution_subtract_fusion.1), custom_call_target="Cholesky" | custom-call | tf_op jit(solution)/shard_map/jit(cholesky)/cholesky | solution.py:20
  375.4 5.3 while.1
  375.4 0.6 fusion.27
  376.0 2.0 bitcast_dynamic-update-slice_fusion.2
  378.0 0.6 fusion.27
  378.6 2.0 bitcast_dynamic-update-slice_fusion.2
  380.7 40.1 %custom-call.19 = f32[2,2,128,128]{2,3,1,0:T(8,128)S(1)} custom-call(f32[2,2,128,128]{3,2,1,0:T(8,128)} %bitcast.49), custom_call_target="InvertDiagBlocksLowerTriangular" | custom-call | tf_op jit(solution)/shard_map/triangular_solve | solution.py:21
  420.8 0.4 fusion.20
  421.2 0.4 convolution_subtract_fusion
  421.6 0.4 convolution_convert_fusion
  422.4 1.3 copy.49
  423.8 1.3 dynamic-slice.4
  425.8 115.6 %all-reduce.13.cloned.1.call-done = f32[512,2,256]{2,1,0:T(2,128)} async-done(((f32[512,2,256]{2,1,0:T(2,128)}), f32[512,2,256]{2,1,0:T(2,128)}) %all-reduce.13.cloned.1.call-update) | async-done | bytes 1048592
  541.3 1.5 constant_dynamic-slice_fusion.1
  542.8 150.3 %all-reduce.11.cloned.1.call-done = f32[32,2,256]{2,1,0:T(2,128)} async-done(((f32[32,2,256]{2,1,0:T(2,128)}), f32[32,2,256]{2,1,0:T(2,128)}) %all-reduce.11.cloned.1.call-update) | async-done | bytes 65552 | tf_op jit(solution)/shard_map/psum | solution.py:47
  693.2 1.5 fusion.18
  694.7 23.0 %all_gather.7 = bf16[512,2,256]{2,1,0:T(2,128)(2,1)S(1)} all-gather(bf16[32,2,256]{2,1,0:T(2,128)(2,1)S(1)} %get-tuple-element.26), channel_id=1, replica_groups=mesh['rep'=32,'fsdp'=16] {'fsdp'}, dimensions={0}, use_global_device_ids=true | all-gather | bytes 557056 | tf_op jit(solution)/shard_map/all_gather | solution.py:48
  717.7 1.8 multiply_subtract_fusion
  (39 shorter events, 1.8 us)
Async XLA Ops:
  7.2 24.1 %copy-start = (bf16[1,2,256,512]{3,2,1,0:T(8,128)(2,1)S(1)}, bf16[1,2,256,512]{3,2,1,0:T(8,128)(2,1)}, u32[]{:S(2)}) copy-start(bf16[1,2,256,512]{3,2,1,0:T(8,128)(2,1)} %param.5) | copy-start | bytes 1572868
  7.2 179.3 %all-reduce.7.cloned.1.call-start = ((), (), s32[]{:S(2)}) async-start(), calls=%async_computation | async-start | bytes 1048576 | tf_op jit(solution)/shard_map/psum | solution.py:38
  32.4 272.8 %all-reduce.9.cloned.1.call-start = ((), (), s32[]{:S(2)}) async-start(), calls=%async_computation.1 | async-start | bytes 1048576 | tf_op jit(solution)/shard_map/psum | solution.py:39
  32.6 0.7 copy-start.5
  189.2 1.0 copy-start.1
  189.2 352.1 %all-reduce.13.cloned.1.call-start = ((), (), s32[]{:S(2)}) async-start(), calls=%async_computation.3 | async-start | bytes 2097152
  306.4 1.0 copy-start.2
  422.4 295.3 %copy-start.4 = (f32[2,256,512]{2,1,0:T(8,128)S(1)}, f32[2,256,512]{2,1,0:T(8,128)}, u32[]{:S(2)}) copy-start(f32[2,256,512]{2,1,0:T(8,128)} %param.7) | copy-start | bytes 3145732
  423.7 294.0 %copy-start.3 = (f32[2,256,512]{2,1,0:T(8,128)S(1)}, f32[2,256,512]{2,1,0:T(8,128)}, u32[]{:S(2)}) copy-start(f32[2,256,512]{2,1,0:T(8,128)} %param.6) | copy-start | bytes 3145732
  423.7 269.5 %all-reduce.11.cloned.1.call-start = ((), (), s32[]{:S(2)}) async-start(), calls=%async_computation.2 | async-start | bytes 131072 | tf_op jit(solution)/shard_map/psum | solution.py:47
Sparse Core Ops, SparseCore 0:
  32.6 153.8 all-reduce.6
  189.5 115.7 all-reduce.8
  423.8 117.4 all-reduce.12
  545.6 147.5 all-reduce.10
where the time goes:
time: 727 us; the launch traced here: 726 us
  waiting for transfers between devices  534 us (73%)
  other arithmetic  112 us (15%)
  blocking collectives  45.4 us (6%)
  between operations  14.6 us (2%)
  local copies, waits for them, and re-layouts  12.1 us (2%)
  matrix products  7.8 us (1%)
    psum x1, waiting for transfers between devices, shards(): left_factor = lax.psum(partial_left, 'rep') / replicas  153 us
    psum x1, waiting for transfers between devices, shards(): new_factors = lax.psum(column_share, 'rep') / replicas  150 us
    unnamed x5, waiting for transfers between devices  116 us
    psum x1, waiting for transfers between devices, shards(): gram_matrix = lax.psum(gram_of(left_factor), 'fsdp') + filler  115 us
    another operation x9, other arithmetic, orthonormal_of(): chol_factor = jnp.linalg.cholesky(gram_matrix)  66.8 us
    another operation x4, other arithmetic, orthonormal_of(): lax.linalg.triangular_solve(chol_factor, factor, left_side=False, lower=T...  40.3 us
    all_gather x1, blocking collectives, shards(): lax.all_gather(new_factors.astype(jnp.bfloat16), 'fsdp', axis=0, tiled=True)  23 us
    all_gather x1, blocking collectives, shards(): warm_full = lax.all_gather(warm, 'fsdp', axis=0, tiled=True)  22.4 us
  transfers between devices with their start and end apart: 4, of which 4 were waited for; matrix products, arithmetic and copies ran while one was open for 0% of the time, Pallas kernels for 0%

commit v1 on v0

v1 whole, which is shorter than its diff:
```python
import jax
import jax.numpy as jnp
from jax import lax
from jax.experimental import pallas as pl
from jax.experimental.pallas import tpu as pltpu
from jax.sharding import PartitionSpec as P

OUTER_RATE = 0.7
OUTER_MOMENTUM = 0.9
MESH = pl.DeviceIdType.MESH
HIGH = lax.Precision.HIGHEST
F32 = jnp.float32
BF16 = jnp.bfloat16
NX, NZ, NY = 4, 8, 8
NREP = NX * NZ
ROWS, COLS, RANK = 256, 512, 256
CH = 16
VMEM = pl.BlockSpec(memory_space=pltpu.VMEM)
REP_STEPS = [(dx, dz) for dx in range(NX) for dz in range(NZ) if (dx, dz) != (0, 0)]
NP = len(REP_STEPS)


def position():
    rep, fsdp = lax.axis_index("rep"), lax.axis_index("fsdp")
    return rep // NZ, rep % NZ, fsdp // 2, fsdp % 2


def split3(x):
    high = x.astype(BF16)
    rest = x - high.astype(F32)
    mid = rest.astype(BF16)
    low = (rest - mid.astype(F32)).astype(BF16)
    return high, mid, low


def outer_rows(a, b):
    ah, am, al = split3(a)
    bh, bm, bl = split3(b)
    left = jnp.concatenate([ah, ah, am, ah, al, am], 0)
    right = jnp.concatenate([bh, bm, bh, bl, bh, bm], 0)
    return lax.dot_general(left, right, (((0,), (0,)), ((), ())), preferred_element_type=F32)


def dot_nt(a, b, precision=HIGH):
    return lax.dot_general(a, b, (((1,), (1,)), ((), ())), precision=precision, preferred_element_type=F32)


def reduce_kernel(
    ranks_ref, deltas_ref, warm_ref,
    mfull, left_out, wfull,
    dbuf, recv_d, wtmp, mpart, recv_m, recv_y, mrow, lrow, leftbuf, send, recv, local_sem,
):
    x, z, y, c = position()
    rep = x * NZ + z
    other = 1 - c

    def at(dx, dz):
        return lax.rem(x + dx, NX) * NZ + lax.rem(z + dz, NZ)

    here = y * 2 + c
    sibling = (rep, y * 2 + other)
    columns = [(rep, lax.rem(y + d, NY) * 2 + c) for d in range(1, NY)]
    replicas = [(at(dx, dz), here) for dx, dz in REP_STEPS]

    barrier = pltpu.get_barrier_semaphore()
    for device in [sibling] + columns + replicas:
        pl.semaphore_signal(barrier, inc=1, device_id=device, device_id_type=MESH)

    lane = lax.broadcasted_iota(jnp.int32, (32, RANK), 1)
    for m in range(2):
        mask = jnp.where(lane < ranks_ref[m], 1.0, 0.0).astype(BF16)
        wtmp[m] = warm_ref[:, m, :].astype(BF16) * mask

    count = [0]
    sends = []

    def push(src, dst, device):
        k = count[0]
        count[0] += 1
        copy = pltpu.make_async_remote_copy(
            src_ref=src, dst_ref=dst, send_sem=send.at[k], recv_sem=recv.at[k],
            device_id=device, device_id_type=MESH,
        )
        copy.start()
        sends.append(copy)
        return copy

    pl.semaphore_wait(barrier, 1 + len(columns) + len(replicas))

    own = pltpu.make_async_copy(deltas_ref.at[0, c], dbuf.at[pl.ds(c * ROWS, ROWS)], local_sem)
    own.start()
    pair_d = push(deltas_ref.at[0, other], dbuf.at[pl.ds(c * ROWS, ROWS)], sibling)
    pair_w = push(wtmp.at[other], wfull.at[pl.ds(here * 32, 32)], sibling)
    wfull[pl.ds(here * 32, 32), :] = wtmp[c]
    own.wait()
    pair_d.wait_recv()
    copies_d = []
    for k, device in enumerate(replicas):
        copies_d.append(push(dbuf.at[pl.ds(device[0] * CH, CH)], recv_d.at[k], device))
    pair_w.wait_recv()
    mine = pl.ds(y * 64, 64)
    copies_w = [push(wfull.at[mine], wfull.at[mine], device) for device in columns]

    for copy in copies_d:
        copy.wait_recv()
    total = dbuf[pl.ds(rep * CH, CH), :].astype(F32)
    for k in range(NP):
        total = total + recv_d[k].astype(F32)
    mean = total * (1.0 / NREP)
    for copy in copies_w:
        copy.wait_recv()
    parts = jnp.dot(jnp.concatenate(split3(mean), 0), wfull[...], preferred_element_type=F32)
    left = parts[0:CH] + parts[CH : 2 * CH] + parts[2 * CH :]
    lrow[...] = left
    mpart[...] = outer_rows(mean, left)

    copies_m = []
    for k, device in enumerate(replicas):
        copies_m.append(push(mpart.at[pl.ds(device[0] * CH, CH)], recv_m.at[k], device))
    mine = pl.ds(rep * CH, CH)
    copies_l = [push(lrow, leftbuf.at[mine], device) for device in replicas]
    leftbuf[mine, :] = left

    for copy in copies_m:
        copy.wait_recv()
    total = mpart[mine, :]
    for k in range(NP):
        total = total + recv_m[k]
    mrow[...] = total
    copies_y = [push(mrow, recv_y.at[k], device) for k, device in enumerate(columns)]
    for copy in copies_y:
        copy.wait_recv()
    for k in range(NY - 1):
        total = total + recv_y[k]
    mfull[mine, :] = total
    copies_f = [push(mfull.at[mine], mfull.at[mine], device) for device in replicas]
    for copy in copies_l:
        copy.wait_recv()
    pair_l = push(leftbuf.at[pl.ds(other * ROWS, ROWS)], left_out.at[c], sibling)
    left_out[c] = leftbuf[pl.ds(c * ROWS, ROWS), :]
    for copy in copies_f:
        copy.wait_recv()
    pair_l.wait_recv()
    for copy in sends:
        copy.wait_send()


def reduce_all(ranks, deltas, warm):
    n = 3 + 4 * NP + 2 * (NY - 1)
    return pl.pallas_call(
        reduce_kernel,
        out_shape=(
            jax.ShapeDtypeStruct((COLS, RANK), F32),
            jax.ShapeDtypeStruct((2, ROWS, RANK), F32),
            jax.ShapeDtypeStruct((COLS, RANK), BF16),
        ),
        in_specs=[pl.BlockSpec(memory_space=pltpu.SMEM), pl.BlockSpec(memory_space=pl.ANY), VMEM],
        out_specs=(VMEM, VMEM, VMEM),
        scratch_shapes=[
            pltpu.VMEM((2 * ROWS, COLS), BF16),
            pltpu.VMEM((NP, CH, COLS), BF16),
            pltpu.VMEM((2, 32, RANK), BF16),
            pltpu.VMEM((COLS, RANK), F32),
            pltpu.VMEM((NP, CH, RANK), F32),
            pltpu.VMEM((NY - 1, CH, RANK), F32),
            pltpu.VMEM((CH, RANK), F32),
            pltpu.VMEM((CH, RANK), F32),
            pltpu.VMEM((2 * ROWS, RANK), F32),
            pltpu.SemaphoreType.DMA((n,)),
            pltpu.SemaphoreType.DMA((n,)),
            pltpu.SemaphoreType.DMA,
        ],
        compiler_params=pltpu.CompilerParams(
            collective_id=1, has_side_effects=True, vmem_limit_bytes=32 * 2**20
        ),
        name="reduce_all",
    )(ranks, deltas, warm)


def spread(x):
    return jnp.broadcast_to(x, (8, 128))


def eliminate(tiles, lane0, groups, width):
    sub = lax.broadcasted_iota(jnp.int32, (8, 128), 0)
    pivots = [None] * groups
    for b in range(groups * 8 // width):
        first = b * width // 8
        col = []
        for k in range(width):
            at = lane0 + b * width + k
            col.append([None] * first + [spread(tiles[0][g][:, at : at + 1]) for g in range(first, groups)])
        for j in range(width):
            g0, s = divmod(b * width + j, 8)
            pivot = spread(col[j][g0][s : s + 1, :])
            inverse = 1.0 / pivot
            factor = [None] * groups
            for g in range(g0, groups):
                factor[g] = jnp.where(sub > s, col[j][g], 0.0) if g == g0 else col[j][g]
            for k in range(j + 1, width):
                row = spread(col[k][g0][s : s + 1, :]) * inverse
                for g in range(g0, groups):
                    col[k][g] = col[k][g] - factor[g] * row
            for t in tiles:
                row = spread(t[g0][s : s + 1, :]) * inverse
                for g in range(g0, groups):
                    t[g] = t[g] - factor[g] * row
            pivots[g0] = pivot if s == 0 else jnp.where(sub == s, pivot, pivots[g0])
    for g in range(groups):
        scale = lax.rsqrt(pivots[g])
        for t in tiles:
            t[g] = t[g] * scale


def inverse_cholesky(a_ref):
    n, width = RANK, 32
    groups = width // 8
    for k0 in range(0, n, width):
        t0 = k0 // 128
        cols = list(range(t0, 2)) + [2 + t for t in range((k0 + width - 1) // 128 + 1)]
        rows = [slice(k0 + 8 * g, k0 + 8 * g + 8) for g in range(groups)]
        tiles = [[a_ref[r, 128 * t : 128 * t + 128] for r in rows] for t in cols]
        eliminate(tiles, k0 % 128, groups, 16)
        for i, t in enumerate(cols):
            for g, r in enumerate(rows):
                a_ref[r, 128 * t : 128 * t + 128] = tiles[i][g]
        if k0 + width < n:
            lo, hi = 128 * cols[0], 128 * cols[-1] + 128
            update = outer_rows(a_ref[k0 : k0 + width, 128 * t0 : n], a_ref[k0 : k0 + width, lo:hi])
            a_ref[k0 + width : n, lo:hi] = a_ref[k0 + width : n, lo:hi] - update[k0 + width - 128 * t0 :, :]


def factor_kernel(ranks_ref, mfull, wfull, linv, factors, factors_b, a_ref):
    core = lax.axis_index("fsdp") % 2
    rank = jnp.where(core == 0, ranks_ref[0], ranks_ref[1])
    m = mfull[...]
    three = lax.dot_general(
        wfull[...], jnp.concatenate(split3(m), 1), (((0,), (0,)), ((), ())), preferred_element_type=F32
    )
    gram = three[:, 0:RANK] + three[:, RANK : 2 * RANK] + three[:, 2 * RANK :]
    row = lax.broadcasted_iota(jnp.int32, (RANK, RANK), 0)
    column = lax.broadcasted_iota(jnp.int32, (RANK, RANK), 1)
    diagonal = row == column
    a_ref[:, 0:RANK] = gram + jnp.where(diagonal & (column >= rank), 1.0, 0.0)
    a_ref[:, RANK:] = jnp.where(diagonal, 1.0, 0.0).astype(F32)
    inverse_cholesky(a_ref)
    inverse = a_ref[:, RANK:]
    linv[...] = inverse
    new = dot_nt(m, inverse)
    factors[...] = new
    factors_b[...] = new.astype(BF16)


def factor_one(ranks, mfull, wfull):
    return pl.pallas_call(
        factor_kernel,
        out_shape=(
            jax.ShapeDtypeStruct((RANK, RANK), F32),
            jax.ShapeDtypeStruct((COLS, RANK), F32),
            jax.ShapeDtypeStruct((COLS, RANK), BF16),
        ),
        in_specs=[pl.BlockSpec(memory_space=pltpu.SMEM), VMEM, VMEM],
        out_specs=(VMEM, VMEM, VMEM),
        scratch_shapes=[pltpu.VMEM((RANK, 2 * RANK), F32)],
        compiler_params=pltpu.CompilerParams(vmem_limit_bytes=32 * 2**20),
        name="factor_one",
    )(ranks, mfull, wfull)


def swap_kernel(linv, factors, factors_b, linv_all, piece_all, factors_all, send, recv):
    rep, here = lax.axis_index("rep"), lax.axis_index("fsdp")
    core = here % 2
    other = here + 1 - 2 * core
    sibling = (rep, other)
    barrier = pltpu.get_barrier_semaphore()
    pl.semaphore_signal(barrier, inc=1, device_id=sibling, device_id_type=MESH)
    pl.semaphore_wait(barrier, 1)
    pairs = (
        (linv, linv_all.at[core]),
        (factors_b, factors_all.at[core]),
        (factors.at[pl.ds(other * 32, 32)], piece_all.at[core]),
    )
    copies = []
    for k, (src, dst) in enumerate(pairs):
        copy = pltpu.make_async_remote_copy(
            src_ref=src, dst_ref=dst, send_sem=send.at[k], recv_sem=recv.at[k],
            device_id=sibling, device_id_type=MESH,
        )
        copy.start()
        copies.append(copy)
    linv_all[core] = linv[...]
    factors_all[core] = factors_b[...]
    piece_all[core] = factors[pl.ds(here * 32, 32), :]
    for copy in copies:
        copy.wait()


def swap(linv, factors, factors_b):
    return pl.pallas_call(
        swap_kernel,
        out_shape=(
            jax.ShapeDtypeStruct((2, RANK, RANK), F32),
            jax.ShapeDtypeStruct((2, 32, RANK), F32),
            jax.ShapeDtypeStruct((2, COLS, RANK), BF16),
        ),
        in_specs=[VMEM] * 3,
        out_specs=(VMEM,) * 3,
        scratch_shapes=[pltpu.SemaphoreType.DMA((3,)), pltpu.SemaphoreType.DMA((3,))],
        compiler_params=pltpu.CompilerParams(
            collective_id=2, has_side_effects=True, vmem_limit_bytes=32 * 2**20
        ),
        name="swap",
    )(linv, factors, factors_b)


def update_kernel(left, linv, factors_b, piece, weights, momentum, new_weights, new_momentum, new_factors):
    for m in range(2):
        orth = dot_nt(left[m], linv[m]).astype(BF16)
        approx = dot_nt(orth, factors_b[m], None)
        fresh = OUTER_MOMENTUM * momentum[m] + approx
        new_momentum[m] = fresh
        new_weights[m] = weights[m] - OUTER_RATE * (approx + OUTER_MOMENTUM * fresh)
        new_factors[:, m, :] = piece[m]


def update(left, linv, factors_b, piece, weights, momentum):
    return pl.pallas_call(
        update_kernel,
        out_shape=(
            jax.ShapeDtypeStruct((2, ROWS, COLS), F32),
            jax.ShapeDtypeStruct((2, ROWS, COLS), F32),
            jax.ShapeDtypeStruct((32, 2, RANK), F32),
        ),
        in_specs=[VMEM] * 6,
        out_specs=(VMEM,) * 3,
        compiler_params=pltpu.CompilerParams(vmem_limit_bytes=32 * 2**20),
        name="update",
    )(left, linv, factors_b, piece, weights, momentum)


def shards(deltas, weights, momentum, warm_factors, matrix_ranks):
    mfull, left, wfull = reduce_all(matrix_ranks, deltas, warm_factors)
    linv, factors, factors_b = factor_one(matrix_ranks, mfull, wfull)
    linv_all, piece, factors_all = swap(linv, factors, factors_b)
    return update(left, linv_all, factors_all, piece, weights, momentum)


def solution(mesh):
    placed = (
        P("rep", None, "fsdp", None),
        P(None, "fsdp", None),
        P(None, "fsdp", None),
        P("fsdp", None, None),
        P(),
    )
    return jax.shard_map(
        shards,
        mesh=mesh,
        in_specs=placed,
        out_specs=(P(None, "fsdp", None), P(None, "fsdp", None), P("fsdp", None, None)),
        check_vma=False,
    )
```

time: 727 us -> 89.6 us (0.12)
  waiting for transfers between devices: 534 us -> 0 us
  other arithmetic: 112 us -> 0 us
  Pallas kernels: 0 us -> 86.1 us
  blocking collectives: 45.4 us -> 0 us
  between operations: 14.6 us -> 0.69 us
  local copies, waits for them, and re-layouts: 12.1 us -> 2.54 us
  matrix products: 7.8 us -> 0 us
    psum x3 -> x0, waiting for transfers between devices: 419 us -> none  [the longest x1 153 us: shards(): left_factor = lax.psum(partial_left, 'rep') / replicas]
    unnamed x5 -> x0, waiting for transfers between devices: 116 us -> none
    another operation x13 -> x0, other arithmetic: 107 us -> none  [the longest x9 66.8 us: orthonormal_of(): chol_factor = jnp.linalg.cholesky(gram_matrix)]
    pallas_call x0 -> x4, Pallas kernels: none -> 86.1 us  [the longest x1 70 us: reduce_all(): pl.pallas_call(reduce_kernel, out_shape=(jax.ShapeDtypeStruct((COLS, RANK...]
    all_gather x2 -> x0, blocking collectives: 45.4 us -> none  [the longest x1 23 us: shards(): lax.all_gather(new_factors.astype(jnp.bfloat16), 'fsdp', axis=0, tiled=True)]
  transfers between devices with their start and end apart: 4 -> 0, of which waited for: 4 -> 0; matrix products, arithmetic and copies ran while one was open for 0% -> 0% of each run, Pallas kernels for 0% -> 0%
where the time goes in v1:
time: 89.6 us; the launch traced here: 89.4 us
  Pallas kernels  86.1 us (96%)
  local copies, waits for them, and re-layouts  2.54 us (3%)
    pallas_call x1, Pallas kernels, reduce_all(): pl.pallas_call(reduce_kernel, out_shape=(jax.ShapeDtypeStruct((COLS, RANK...  70 us
    pallas_call x1, Pallas kernels, factor_one(): pl.pallas_call(factor_kernel, out_shape=(jax.ShapeDtypeStruct((RANK, RANK...  8 us
    pallas_call x1, Pallas kernels, swap(): pl.pallas_call(swap_kernel, out_shape=(jax.ShapeDtypeStruct((2, RANK, RAN...  5.42 us
    pallas_call x1, Pallas kernels, update(): pl.pallas_call(update_kernel, out_shape=(jax.ShapeDtypeStruct((2, ROWS, C...  2.76 us
    unnamed x10, local copies, waits for them, and re-layouts  2.54 us

profile of v1, /device:TPU:1, one launch (start us, length us, event | category | flops | bytes accessed | tf_op | source)
XLA Modules:
  0.0 89.4 jit_solution(11669565046868052439)
XLA Ops:
  0.6 0.0 copy-start.2
  0.6 1.0 %copy-done.2 = bf16[1,2,256,512]{3,2,1,0:T(8,128)(2,1)S(1)} copy-done((bf16[1,2,256,512]{3,2,1,0:T(8,128)(2,1)S(1)}, bf16[1,2,256,512]{3,2,1,0:T(8,128)(2,1)}, u32[]{:S(2)}) %copy-start.2) | copy-done | bytes 524312
  1.7 0.0 copy-start.3
  1.7 0.8 copy-done.3
  2.5 0.0 copy-start.4
  2.5 0.7 copy-done.4
  3.2 0.0 copy-start.1
  3.2 70.0 %reduce_all.1 = (f32[512,256]{1,0:T(8,128)S(1)}, f32[2,256,256]{2,1,0:T(8,128)S(1)}, bf16[512,256]{1,0:T(8,128)(2,1)S(1)}) custom-call(s32[2]{0:T(128)S(1)} %copy-done.4, bf16[1,2,256,512]{3,2,1,0:T(8,128)(2,1)S(1)} %copy-done.2, f32[32,2,256]{2,1,0:T(2,128)S(1)} %copy-done.3), custom_call_target="tpu_custom_call" | custom-call | tf_op jit(solution)/shard_map/reduce_all/pallas_call | solution.py:150
  73.2 0.0 copy-start
  73.2 8.0 %factor_one.1 = (f32[256,256]{1,0:T(8,128)S(1)}, f32[512,256]{1,0:T(8,128)S(1)}, bf16[512,256]{1,0:T(8,128)(2,1)S(1)}) custom-call(s32[2]{0:T(128)S(1)} %copy-done.4, f32[512,256]{1,0:T(8,128)S(1)} %get-tuple-element.13.mfull, bf16[512,256]{1,0:T(8,128)(2,1)S(1)} %get-tuple-element.14.wfull), custom_call_target="tpu_custom_call" | custom-call | tf_op jit(solution)/shard_map/factor_one/pallas_call | solution.py:255
  81.2 5.4 %swap.1 = (f32[2,256,256]{2,1,0:T(8,128)S(1)}, f32[2,32,256]{2,1,0:T(8,128)S(1)}, bf16[2,512,256]{2,1,0:T(8,128)(2,1)S(1)}) custom-call(f32[256,256]{1,0:T(8,128)S(1)} %get-tuple-element.15.linv, f32[512,256]{1,0:T(8,128)S(1)} %get-tuple-element.16.factors, bf16[512,256]{1,0:T(8,128)(2,1)S(1)} %get-tuple-element.17.factors_b), custom_call_target="tpu_custom_call" | custom-call | tf_op jit(solution)/shard_map/swap/pallas_call | solution.py:299
  86.6 0.0 copy-done.1
  86.6 0.0 copy-done
  86.6 2.8 %update.1 = (f32[2,256,512]{2,1,0:T(8,128)}, f32[2,256,512]{2,1,0:T(8,128)}, f32[32,2,256]{2,1,0:T(2,128)}) custom-call(f32[2,256,256]{2,1,0:T(8,128)S(1)} %get-tuple-element.12.left, f32[2,256,256]{2,1,0:T(8,128)S(1)} %get-tuple-element.18.linv, bf16[2,512,256]{2,1,0:T(8,128)(2,1)S(1)} %get-tuple-element.19.factors_b, ...), custom_call_target="tpu_custom_call" | custom-call | tf_op jit(solution)/shard_map/update/pallas_call | solution.py:327
Async XLA Ops:
  0.6 1.0 %copy-start.2 = (bf16[1,2,256,512]{3,2,1,0:T(8,128)(2,1)S(1)}, bf16[1,2,256,512]{3,2,1,0:T(8,128)(2,1)}, u32[]{:S(2)}) copy-start(bf16[1,2,256,512]{3,2,1,0:T(8,128)(2,1)} %deltas_ref.1) | copy-start | bytes 1572868
  1.7 0.8 copy-start.3
  2.5 0.7 copy-start.4
  3.2 83.4 %copy-start.1 = (f32[2,256,512]{2,1,0:T(8,128)S(1)}, f32[2,256,512]{2,1,0:T(8,128)}, u32[]{:S(2)}) copy-start(f32[2,256,512]{2,1,0:T(8,128)} %momentum.1) | copy-start | bytes 3145732
  73.2 13.5 %copy-start = (f32[2,256,512]{2,1,0:T(8,128)S(1)}, f32[2,256,512]{2,1,0:T(8,128)}, u32[]{:S(2)}) copy-start(f32[2,256,512]{2,1,0:T(8,128)} %weights.1) | copy-start | bytes 3145732

commit v2 on v0

v2 whole, which is shorter than its diff:
```python
import jax
import jax.numpy as jnp
from jax import lax
from jax.experimental import pallas as pl
from jax.experimental.pallas import tpu as pltpu
from jax.sharding import PartitionSpec as P

OUTER_RATE = 0.7
OUTER_MOMENTUM = 0.9
MESH = pl.DeviceIdType.MESH
HIGH = lax.Precision.HIGHEST
F32 = jnp.float32
BF16 = jnp.bfloat16
NX, NZ, NY = 4, 8, 8
NREP = NX * NZ
ROWS, COLS, RANK = 256, 512, 256
CH = 16
HALF = RANK // 2
VMEM = pl.BlockSpec(memory_space=pltpu.VMEM)
IN_HBM = pl.BlockSpec(memory_space=pltpu.HBM)
REP_STEPS = [(dx, dz) for dx in range(NX) for dz in range(NZ) if (dx, dz) != (0, 0)]


def position():
    rep, fsdp = lax.axis_index("rep"), lax.axis_index("fsdp")
    return rep // NZ, rep % NZ, fsdp // 2, fsdp % 2


def split3(x):
    high = x.astype(BF16)
    rest = x - high.astype(F32)
    mid = rest.astype(BF16)
    low = (rest - mid.astype(F32)).astype(BF16)
    return high, mid, low


def outer_rows(a, b):
    ah, am, al = split3(a)
    bh, bm, bl = split3(b)
    left = jnp.concatenate([ah, ah, am, ah, al, am], 0)
    right = jnp.concatenate([bh, bm, bh, bl, bh, bm], 0)
    return lax.dot_general(left, right, (((0,), (0,)), ((), ())), preferred_element_type=F32)


def dot_nt(a, b, precision=HIGH):
    return lax.dot_general(a, b, (((1,), (1,)), ((), ())), precision=precision, preferred_element_type=F32)


def spread(x):
    return jnp.broadcast_to(x, (8, 128))


def eliminate(tiles, lane0, groups, width):
    sub = lax.broadcasted_iota(jnp.int32, (8, 128), 0)
    pivots = [None] * groups
    for b in range(groups * 8 // width):
        first = b * width // 8
        col = []
        for k in range(width):
            at = lane0 + b * width + k
            col.append([None] * first + [spread(tiles[0][g][:, at : at + 1]) for g in range(first, groups)])
        for j in range(width):
            g0, s = divmod(b * width + j, 8)
            pivot = spread(col[j][g0][s : s + 1, :])
            inverse = 1.0 / pivot
            factor = [None] * groups
            for g in range(g0, groups):
                factor[g] = jnp.where(sub > s, col[j][g], 0.0) if g == g0 else col[j][g]
            for k in range(j + 1, width):
                row = spread(col[k][g0][s : s + 1, :]) * inverse
                for g in range(g0, groups):
                    col[k][g] = col[k][g] - factor[g] * row
            for t in tiles:
                row = spread(t[g0][s : s + 1, :]) * inverse
                for g in range(g0, groups):
                    t[g] = t[g] - factor[g] * row
            pivots[g0] = pivot if s == 0 else jnp.where(sub == s, pivot, pivots[g0])
    for g in range(groups):
        scale = lax.rsqrt(pivots[g])
        for t in tiles:
            t[g] = t[g] * scale


def eliminate_rows(a_ref, start, stop):
    width = 32
    groups = width // 8
    for k0 in range(start, stop, width):
        t0 = k0 // 128
        cols = list(range(t0, 2)) + [2 + t for t in range((k0 + width - 1) // 128 + 1)]
        rows = [slice(k0 + 8 * g, k0 + 8 * g + 8) for g in range(groups)]
        tiles = [[a_ref[r, 128 * t : 128 * t + 128] for r in rows] for t in cols]
        eliminate(tiles, k0 % 128, groups, 16)
        for i, t in enumerate(cols):
            for g, r in enumerate(rows):
                a_ref[r, 128 * t : 128 * t + 128] = tiles[i][g]
        if k0 + width < stop:
            lo, hi = 128 * cols[0], 128 * cols[-1] + 128
            block = slice(128 * t0, 128 * t0 + 128)
            update = outer_rows(a_ref[k0 : k0 + width, block], a_ref[k0 : k0 + width, lo:hi])
            a_ref[k0 + width : stop, lo:hi] = a_ref[k0 + width : stop, lo:hi] - update[k0 + width - 128 * t0 :, :]


def three_part_tn(a, b):
    n = a.shape[1]
    out = lax.dot_general(
        jnp.concatenate(split3(a), 1), b, (((0,), (0,)), ((), ())), preferred_element_type=F32
    )
    return out[0:n] + out[n : 2 * n] + out[2 * n :]


def factor_kernel(
    ranks_hbm, deltas_hbm, warm_hbm,
    orth_all, factors_all, piece_all,
    ranks_ref, warm_ref, dbuf, recv_d, wtmp, wfull, mpart, recv_m, recv_y, mrow, mfull, lrow, leftbuf, a_ref, obuf,
    factors, local, send, sem_d, sem_m, sem_y, sem_f, sem_lz, sem_lx, sem_w, sem_p,
):
    x, z, y, c = position()
    rep = x * NZ + z
    other = 1 - c
    here = y * 2 + c
    there = y * 2 + other

    def at(dx, dz):
        return lax.rem(x + dx, NX) * NZ + lax.rem(z + dz, NZ)

    sibling = (rep, there)
    columns = [(rep, lax.rem(y + d, NY) * 2 + c) for d in range(1, NY)]
    along_z = [(at(0, dz), here) for dz in range(1, NZ)]
    along_x = [(at(dx, 0), here) for dx in range(1, NX)]
    replicas = [(at(dx, dz), here) for dx, dz in REP_STEPS]

    local_copies = [
        pltpu.make_async_copy(ranks_hbm, ranks_ref, local.at[0]),
        pltpu.make_async_copy(warm_hbm, warm_ref, local.at[1]),
        pltpu.make_async_copy(deltas_hbm.at[0, c], dbuf.at[pl.ds(c * ROWS, ROWS)], local.at[2]),
    ]
    for copy in local_copies:
        copy.start()
    barrier = pltpu.get_barrier_semaphore()
    for device in replicas + columns + [sibling]:
        pl.semaphore_signal(barrier, inc=1, device_id=device, device_id_type=MESH)

    sends = []

    def remote(src, dst, sem, device):
        return pltpu.make_async_remote_copy(
            src_ref=src, dst_ref=dst, send_sem=send.at[len(sends)], recv_sem=sem,
            device_id=device, device_id_type=MESH,
        )

    def push(src, dst, sem, device):
        copy = remote(src, dst, sem, device)
        copy.start()
        sends.append(copy)
        return copy

    for copy in local_copies:
        copy.wait()
    lane = lax.broadcasted_iota(jnp.int32, (32, RANK), 1)
    for m in range(2):
        mask = jnp.where(lane < ranks_ref[m], 1.0, 0.0).astype(BF16)
        wtmp[m] = warm_ref[:, m, :].astype(BF16) * mask
    wfull[pl.ds(here * 32, 32), :] = wtmp[c]
    pl.semaphore_wait(barrier, len(replicas) + len(columns) + 1)

    pair_d = push(deltas_hbm.at[0, other], dbuf.at[pl.ds(c * ROWS, ROWS)], sem_p.at[0], sibling)
    pair_w = push(wtmp.at[other], wfull.at[pl.ds(here * 32, 32)], sem_p.at[1], sibling)

    def push_d(x_to, dz):
        to = x_to * NZ + lax.rem(z + dz, NZ)
        slot = lax.rem(x_to - x + NX, NX) * NZ + dz
        push(dbuf.at[pl.ds(to * CH, CH)], recv_d.at[slot], sem_d.at[slot], (to, here))

    for dz in range(1, NZ):
        for step in range(2):
            push_d(2 * c + step, dz)
    pair_w.wait_recv()
    mine = pl.ds(y * 64, 64)
    copies_w = [push(wfull.at[mine], wfull.at[mine], sem_w.at[k], to) for k, to in enumerate(columns)]
    pair_d.wait_recv()
    for dz in range(1, NZ):
        for step in range(2):
            push_d(2 * other + step, dz)
    for dx in range(1, NX):
        push_d(lax.rem(x + dx, NX), 0)

    mine = pl.ds(rep * CH, CH)
    total = dbuf[mine, :].astype(F32)
    for dx, dz in REP_STEPS:
        slot = dx * NZ + dz
        remote(recv_d.at[slot], recv_d.at[slot], sem_d.at[slot], sibling).wait_recv()
        total = total + recv_d[slot].astype(F32)
    mean = total * (1.0 / NREP)
    for copy in copies_w:
        copy.wait_recv()
    parts = jnp.dot(jnp.concatenate(split3(mean), 0), wfull[...], preferred_element_type=F32)
    left = parts[0:CH] + parts[CH : 2 * CH] + parts[2 * CH :]

    copies_m = [[], []]
    for h in range(2):
        mpart[h] = outer_rows(mean, left[:, h * HALF : h * HALF + HALF])
        for k, to in enumerate(replicas):
            src = mpart.at[h, pl.ds(to[0] * CH, CH)]
            copies_m[h].append(push(src, recv_m.at[h, k], sem_m.at[h, k], to))
    lrow[...] = left
    leftbuf[mine, :] = left
    copies_lz = [push(lrow, leftbuf.at[mine], sem_lz.at[k], to) for k, to in enumerate(along_z)]

    totals = [None, None]
    copies_y = [None, None]
    for h in range(2):
        total = mpart[h, mine, :]
        for k, copy in enumerate(copies_m[h]):
            copy.wait_recv()
            total = total + recv_m[h, k]
        mrow[h] = total
        copies_y[h] = [push(mrow.at[h], recv_y.at[h, k], sem_y.at[h, k], to) for k, to in enumerate(columns)]
        totals[h] = total
    copies_f = [None, None]
    copies_lx = None
    for h in range(2):
        total = totals[h]
        for k, copy in enumerate(copies_y[h]):
            copy.wait_recv()
            total = total + recv_y[h, k]
        mfull[h, mine, :] = total
        src = mfull.at[h, mine]
        copies_f[h] = [push(src, src, sem_f.at[h, k], to) for k, to in enumerate(replicas)]
        if h == 0:
            for copy in copies_lz:
                copy.wait_recv()
            src = leftbuf.at[pl.ds(x * NZ * CH, NZ * CH)]
            copies_lx = [push(src, src, sem_lx.at[k], to) for k, to in enumerate(along_x)]

    row = lax.broadcasted_iota(jnp.int32, (HALF, RANK), 0)
    column = lax.broadcasted_iota(jnp.int32, (HALF, RANK), 1)
    rank = jnp.where(c == 0, ranks_ref[0], ranks_ref[1])
    identity = jnp.where(row == column, 1.0, 0.0).astype(F32)[:, 0:HALF]
    rest = pl.ds(HALF, HALF)

    for copy in copies_f[0]:
        copy.wait_recv()
    filler = jnp.where((row == column) & (column >= rank), 1.0, 0.0)
    a_ref[0:HALF, 0:RANK] = three_part_tn(mfull[0], wfull[...]) + filler
    a_ref[0:HALF, RANK : RANK + HALF] = identity
    eliminate_rows(a_ref, 0, HALF)
    inverse = a_ref[0:HALF, RANK : RANK + HALF]
    above = lax.dot_general(
        a_ref[0:HALF, HALF:RANK], a_ref[0:HALF, HALF : RANK + HALF],
        (((0,), (0,)), ((), ())), precision=HIGH, preferred_element_type=F32,
    )
    a_ref[HALF:RANK, RANK : RANK + HALF] = 0.0 - above[:, HALF:RANK]
    a_ref[HALF:RANK, RANK + HALF :] = identity

    pairs = []

    def finish(h, new, orth):
        cols = slice(h * HALF, h * HALF + HALF)
        factors[:, cols] = new
        factors_all[c, h] = new.astype(BF16)
        obuf[h] = orth.astype(BF16)
        orth_all[c, h] = obuf[h, pl.ds(c * ROWS, ROWS), :]
        src = factors_all.at[c, h]
        pairs.append(push(src, src, sem_p.at[2 + 2 * h], sibling))
        src = obuf.at[h, pl.ds(other * ROWS, ROWS)]
        pairs.append(push(src, orth_all.at[c, h], sem_p.at[3 + 2 * h], sibling))

    for copy in copies_lx:
        copy.wait_recv()
    finish(0, dot_nt(mfull[0], inverse), dot_nt(leftbuf[:, 0:HALF], inverse))

    for copy in copies_f[1]:
        copy.wait_recv()
    filler = jnp.where((row == column) & (column + HALF >= rank), 1.0, 0.0)[:, 0:HALF]
    a_ref[HALF:RANK, HALF:RANK] = three_part_tn(mfull[1], wfull[:, HALF:]) + filler - above[:, 0:HALF]
    eliminate_rows(a_ref, HALF, RANK)
    inverse = a_ref[HALF:RANK, RANK:]
    new = dot_nt(mfull[0], inverse[:, 0:HALF]) + dot_nt(mfull[1], inverse[:, HALF:])
    finish(1, new, dot_nt(leftbuf[...], inverse))
    pairs.append(push(factors.at[pl.ds(there * 32, 32)], piece_all.at[c], sem_p.at[6], sibling))
    piece_all[c] = factors[pl.ds(here * 32, 32), :]
    for copy in pairs:
        copy.wait_recv()
    for copy in sends:
        copy.wait_send()


def factor_all(ranks, deltas, warm):
    others = len(REP_STEPS)
    total = 2 + others + (NY - 1) + 2 * others + (NZ - 1) + 2 * (NY - 1) + 2 * others + (NX - 1) + 5
    dma = pltpu.SemaphoreType.DMA
    return pl.pallas_call(
        factor_kernel,
        out_shape=(
            jax.ShapeDtypeStruct((2, 2, ROWS, HALF), BF16),
            jax.ShapeDtypeStruct((2, 2, COLS, HALF), BF16),
            jax.ShapeDtypeStruct((2, 32, RANK), F32),
        ),
        in_specs=[IN_HBM] * 3,
        out_specs=(VMEM,) * 3,
        scratch_shapes=[
            pltpu.SMEM((2,), jnp.int32),
            pltpu.VMEM((32, 2, RANK), F32),
            pltpu.VMEM((2 * ROWS, COLS), BF16),
            pltpu.VMEM((NREP, CH, COLS), BF16),
            pltpu.VMEM((2, 32, RANK), BF16),
            pltpu.VMEM((COLS, RANK), BF16),
            pltpu.VMEM((2, COLS, HALF), F32),
            pltpu.VMEM((2, others, CH, HALF), F32),
            pltpu.VMEM((2, NY - 1, CH, HALF), F32),
            pltpu.VMEM((2, CH, HALF), F32),
            pltpu.VMEM((2, COLS, HALF), F32),
            pltpu.VMEM((CH, RANK), F32),
            pltpu.VMEM((2 * ROWS, RANK), F32),
            pltpu.VMEM((RANK, 2 * RANK), F32),
            pltpu.VMEM((2, 2 * ROWS, HALF), BF16),
            pltpu.VMEM((COLS, RANK), F32),
            dma((3,)), dma((total,)), dma((NREP,)), dma((2, others)), dma((2, NY - 1)), dma((2, others)),
            dma((NZ - 1,)), dma((NX - 1,)), dma((NY - 1,)), dma((7,)),
        ],
        compiler_params=pltpu.CompilerParams(
            collective_id=1, has_side_effects=True, vmem_limit_bytes=32 * 2**20
        ),
        name="factor_all",
        cost_estimate=pl.CostEstimate(flops=10**9, bytes_accessed=0, transcendentals=0),
    )(*(pltpu.with_memory_space_constraint(a, pltpu.HBM) for a in (ranks, deltas, warm)))


def update_kernel(orth, factors, piece, weights, momentum, new_weights, new_momentum, new_factors):
    for m in range(2):
        approx = dot_nt(orth[m, 0], factors[m, 0], None) + dot_nt(orth[m, 1], factors[m, 1], None)
        fresh = OUTER_MOMENTUM * momentum[m] + approx
        new_momentum[m] = fresh
        new_weights[m] = weights[m] - OUTER_RATE * (approx + OUTER_MOMENTUM * fresh)
        new_factors[:, m, :] = piece[m]


def update(orth, factors, piece, weights, momentum):
    return pl.pallas_call(
        update_kernel,
        out_shape=(
            jax.ShapeDtypeStruct((2, ROWS, COLS), F32),
            jax.ShapeDtypeStruct((2, ROWS, COLS), F32),
            jax.ShapeDtypeStruct((32, 2, RANK), F32),
        ),
        in_specs=[VMEM] * 5,
        out_specs=(VMEM,) * 3,
        compiler_params=pltpu.CompilerParams(vmem_limit_bytes=32 * 2**20),
        name="update",
    )(orth, factors, piece, weights, momentum)


def shards(deltas, weights, momentum, warm_factors, matrix_ranks):
    orth, factors, piece = factor_all(matrix_ranks, deltas, warm_factors)
    return update(orth, factors, piece, weights, momentum)


def solution(mesh):
    placed = (
        P("rep", None, "fsdp", None),
        P(None, "fsdp", None),
        P(None, "fsdp", None),
        P("fsdp", None, None),
        P(),
    )
    return jax.shard_map(
        shards,
        mesh=mesh,
        in_specs=placed,
        out_specs=(P(None, "fsdp", None), P(None, "fsdp", None), P("fsdp", None, None)),
        check_vma=False,
    )
```

time: 727 us -> 72.9 us (0.10)
  waiting for transfers between devices: 534 us -> 0 us
  other arithmetic: 112 us -> 0 us
  Pallas kernels: 0 us -> 72.1 us
  blocking collectives: 45.4 us -> 0 us
  between operations: 14.6 us -> 0.67 us
  local copies, waits for them, and re-layouts: 12.1 us -> 0.01 us
  matrix products: 7.8 us -> 0 us
    psum x3 -> x0, waiting for transfers between devices: 419 us -> none  [the longest x1 153 us: shards(): left_factor = lax.psum(partial_left, 'rep') / replicas]
    unnamed x5 -> x0, waiting for transfers between devices: 116 us -> none
    another operation x13 -> x0, other arithmetic: 107 us -> none  [the longest x9 66.8 us: orthonormal_of(): chol_factor = jnp.linalg.cholesky(gram_matrix)]
    pallas_call x0 -> x2, Pallas kernels: none -> 72.1 us  [the longest x1 70.3 us: factor_all(): pl.pallas_call(factor_kernel, out_shape=(jax.ShapeDtypeStruct((2, 2, ROWS...]
    all_gather x2 -> x0, blocking collectives: 45.4 us -> none  [the longest x1 23 us: shards(): lax.all_gather(new_factors.astype(jnp.bfloat16), 'fsdp', axis=0, tiled=True)]
  transfers between devices with their start and end apart: 4 -> 0, of which waited for: 4 -> 0; matrix products, arithmetic and copies ran while one was open for 0% -> 0% of each run, Pallas kernels for 0% -> 0%
where the time goes in v2:
time: 72.9 us; the launch traced here: 72.8 us
  Pallas kernels  72.1 us (99%)
    pallas_call x1, Pallas kernels, factor_all(): pl.pallas_call(factor_kernel, out_shape=(jax.ShapeDtypeStruct((2, 2, ROWS...  70.3 us
    pallas_call x1, Pallas kernels, update(): pl.pallas_call(update_kernel, out_shape=(jax.ShapeDtypeStruct((2, ROWS, C...  1.81 us

profile of v2, /device:TPU:1, one launch (start us, length us, event | category | flops | bytes accessed | tf_op | source)
XLA Modules:
  0.0 72.8 jit_solution(18164288531093384910)
XLA Ops:
  0.6 0.0 copy-start.1
  0.6 0.0 copy-start
  0.7 70.3 %factor_all.1 = (bf16[2,2,256,128]{3,2,1,0:T(8,128)(2,1)S(1)}, bf16[2,2,512,128]{3,2,1,0:T(8,128)(2,1)S(1)}, f32[2,32,256]{2,1,0:T(8,128)S(1)}) custom-call(s32[2]{0:T(128)} %ranks_hbm.1, bf16[1,2,256,512]{3,2,1,0:T(8,128)(2,1)} %deltas_hbm.1, f32[32,2,256]{2,1,0:T(2,128)} %warm_hbm.1), custom_call_target="tpu_custom_call" | custom-call | flops 1000000000 | tf_op jit(solution)/shard_map/factor_all/pallas_call | solution.py:292
  71.0 0.0 copy-done.1
  71.0 0.0 copy-done
  71.0 1.8 %update.1 = (f32[2,256,512]{2,1,0:T(8,128)}, f32[2,256,512]{2,1,0:T(8,128)}, f32[32,2,256]{2,1,0:T(2,128)}) custom-call(bf16[2,2,256,128]{3,2,1,0:T(8,128)(2,1)S(1)} %get-tuple-element.6.orth, bf16[2,2,512,128]{3,2,1,0:T(8,128)(2,1)S(1)} %get-tuple-element.7.factors, f32[2,32,256]{2,1,0:T(8,128)S(1)} %get-tuple-element.8.piece, f32[2,256,512]{2,1,0:T(8,128)S(1)} %copy-done, ...), custom_call_target="tpu_custom_call" | custom-call | tf_op jit(solution)/shard_map/update/pallas_call | solution.py:339
Async XLA Ops:
  0.6 70.3 %copy-start.1 = (f32[2,256,512]{2,1,0:T(8,128)S(1)}, f32[2,256,512]{2,1,0:T(8,128)}, u32[]{:S(2)}) copy-start(f32[2,256,512]{2,1,0:T(8,128)} %momentum.1) | copy-start | bytes 3145732
  0.6 70.3 %copy-start = (f32[2,256,512]{2,1,0:T(8,128)S(1)}, f32[2,256,512]{2,1,0:T(8,128)}, u32[]{:S(2)}) copy-start(f32[2,256,512]{2,1,0:T(8,128)} %weights.1) | copy-start | bytes 3145732

commit v3 on v2

v3 whole, which is shorter than its diff:
```python
import jax
import jax.numpy as jnp
from jax import lax
from jax.experimental import pallas as pl
from jax.experimental.pallas import tpu as pltpu
from jax.sharding import PartitionSpec as P

OUTER_RATE = 0.7
OUTER_MOMENTUM = 0.9
MESH = pl.DeviceIdType.MESH
F32 = jnp.float32
BF16 = jnp.bfloat16
NX, NZ, NY = 4, 8, 8
NREP = NX * NZ
ROWS, COLS, RANK = 256, 512, 256
CH = 16
UNIT = 64
UNITS = RANK // UNIT
PIECES = ((0, 128), (128, 256))
PLANES = "zy"
SCHEDULE = "mmyy"
WIDE = COLS + 2 * ROWS
VMEM = pl.BlockSpec(memory_space=pltpu.VMEM)
IN_HBM = pl.BlockSpec(memory_space=pltpu.HBM)
PLANE_STEPS = [(dx, d) for dx in range(NX) for d in range(NY) if dx and d]
REP_STEPS = [(dx, dz) for dx in range(NX) for dz in range(NZ) if (dx, dz) != (0, 0)]


def position():
    rep, fsdp = lax.axis_index("rep"), lax.axis_index("fsdp")
    return rep // NZ, rep % NZ, fsdp // 2, fsdp % 2


def split3(x):
    high = x.astype(BF16)
    rest = x - high.astype(F32)
    mid = rest.astype(BF16)
    low = (rest - mid.astype(F32)).astype(BF16)
    return high, mid, low


def outer_rows(a, b):
    ah, am, al = split3(a)
    bh, bm, bl = split3(b)
    left = jnp.concatenate([ah, ah, am, ah, al, am], 0)
    right = jnp.concatenate([bh, bm, bh, bl, bh, bm], 0)
    return lax.dot_general(left, right, (((0,), (0,)), ((), ())), preferred_element_type=F32)


def six_lanes(a):
    high, mid, low = split3(a)
    return jnp.concatenate([high, high, mid, high, low, mid], 1)


def six_rows(parts):
    high, mid, low = parts
    return jnp.concatenate([high, mid, high, low, high, mid], 0)


def spread(x):
    return jnp.broadcast_to(x, (8, 128))


def eliminate(tiles, lane0, groups, width):
    sub = lax.broadcasted_iota(jnp.int32, (8, 128), 0)
    pivots = [None] * groups
    for b in range(groups * 8 // width):
        first = b * width // 8
        col = []
        for k in range(width):
            at = lane0 + b * width + k
            col.append([None] * first + [spread(tiles[0][g][:, at : at + 1]) for g in range(first, groups)])
        for j in range(width):
            g0, s = divmod(b * width + j, 8)
            pivot = spread(col[j][g0][s : s + 1, :])
            inverse = 1.0 / pivot
            factor = [None] * groups
            for g in range(g0, groups):
                factor[g] = jnp.where(sub > s, col[j][g], 0.0) if g == g0 else col[j][g]
            for k in range(j + 1, width):
                row = spread(col[k][g0][s : s + 1, :]) * inverse
                for g in range(g0, groups):
                    col[k][g] = col[k][g] - factor[g] * row
            for t in tiles:
                row = spread(t[g0][s : s + 1, :]) * inverse
                for g in range(g0, groups):
                    t[g] = t[g] - factor[g] * row
            pivots[g0] = pivot if s == 0 else jnp.where(sub == s, pivot, pivots[g0])
    for g in range(groups):
        scale = lax.rsqrt(pivots[g])
        for t in tiles:
            t[g] = t[g] * scale


def eliminate_rows(a_ref, start, stop):
    width = 32
    groups = width // 8
    for k0 in range(start, stop, width):
        t0 = k0 // 128
        cols = list(range(t0, RANK // 128)) + [RANK // 128]
        rows = [slice(k0 + 8 * g, k0 + 8 * g + 8) for g in range(groups)]
        tiles = [[a_ref[r, 128 * t : 128 * t + 128] for r in rows] for t in cols]
        eliminate(tiles, k0 % 128, groups, 16)
        for i, t in enumerate(cols):
            for g, r in enumerate(rows):
                a_ref[r, 128 * t : 128 * t + 128] = tiles[i][g]
        if k0 + width < stop:
            block = slice(128 * t0, 128 * t0 + 128)
            update = outer_rows(a_ref[k0 : k0 + width, block], a_ref[k0 : k0 + width, 128 * t0 :])
            rest = slice(k0 + width - 128 * t0, stop - 128 * t0)
            a_ref[k0 + width : stop, 128 * t0 :] = a_ref[k0 + width : stop, 128 * t0 :] - update[rest, :]


def factor_kernel(
    ranks_hbm, deltas_hbm, warm_hbm,
    orth_all, factors_all, piece_all,
    ranks_ref, warm_ref, dbuf, recv_d, wtmp, wfull, mpart, recv_m, recv_y, mrow, mfull, lrow, leftbuf, left_t, a_ref,
    solved, obuf, blocks, local, send, sem_d, sem_m, sem_y, sem_f, sem_lz, sem_lx, sem_w, sem_p,
):
    x, z, y, c = position()
    rep = x * NZ + z
    other = 1 - c
    here = y * 2 + c
    there = y * 2 + other

    def at(dx, dz):
        return lax.rem(x + dx, NX) * NZ + lax.rem(z + dz, NZ)

    sibling = (rep, there)
    columns = [(rep, lax.rem(y + d, NY) * 2 + c) for d in range(1, NY)]
    along_z = [(at(0, dz), here) for dz in range(1, NZ)]
    along_x = [(at(dx, 0), here) for dx in range(1, NX)]
    replicas = [(at(dx, dz), here) for dx, dz in REP_STEPS]

    def across(dx, dy):
        return lax.rem(x + dx, NX), lax.rem(y + dy, NY)

    in_xy = [across(dx, dy) for dx, dy in REP_STEPS]
    in_xy = [((to_x * NZ + z, to_y * 2 + c), to_x * NY + to_y) for to_x, to_y in in_xy]
    in_xz = [(device, device[0]) for device in replicas]
    planes = [in_xz if plane == "z" else in_xy for plane in PLANES]
    owned = [rep if plane == "z" else x * NY + y for plane in PLANES]
    lines = [columns if plane == "z" else along_z for plane in PLANES]
    corners = [in_xy[k][0] for k, step in enumerate(REP_STEPS) if step in PLANE_STEPS]

    local_copies = [
        pltpu.make_async_copy(ranks_hbm, ranks_ref, local.at[0]),
        pltpu.make_async_copy(warm_hbm, warm_ref, local.at[1]),
        pltpu.make_async_copy(deltas_hbm.at[0, c], dbuf.at[pl.ds(c * ROWS, ROWS)], local.at[2]),
    ]
    for copy in local_copies:
        copy.start()
    barrier = pltpu.get_barrier_semaphore()
    for device in replicas + columns + corners + [sibling]:
        pl.semaphore_signal(barrier, inc=1, device_id=device, device_id_type=MESH)

    sends = []

    def remote(src, dst, sem, device):
        return pltpu.make_async_remote_copy(
            src_ref=src, dst_ref=dst, send_sem=send.at[len(sends)], recv_sem=sem,
            device_id=device, device_id_type=MESH,
        )

    def push(src, dst, sem, device):
        copy = remote(src, dst, sem, device)
        copy.start()
        sends.append(copy)
        return copy

    for copy in local_copies:
        copy.wait()
    lane = lax.broadcasted_iota(jnp.int32, (32, RANK), 1)
    for m in range(2):
        mask = jnp.where(lane < ranks_ref[m], 1.0, 0.0).astype(BF16)
        wtmp[m] = warm_ref[:, m, :].astype(BF16) * mask
    wfull[pl.ds(here * 32, 32), :] = wtmp[c]
    pl.semaphore_wait(barrier, len(replicas) + len(columns) + len(corners) + 1)

    pair_d = push(deltas_hbm.at[0, other], dbuf.at[pl.ds(c * ROWS, ROWS)], sem_p.at[0], sibling)
    pair_w = push(wtmp.at[other], wfull.at[pl.ds(here * 32, 32)], sem_p.at[1], sibling)

    def push_d(x_to, dz):
        to = x_to * NZ + lax.rem(z + dz, NZ)
        slot = lax.rem(x_to - x + NX, NX) * NZ + dz
        push(dbuf.at[pl.ds(to * CH, CH)], recv_d.at[slot], sem_d.at[slot], (to, here))

    for dz in range(1, NZ):
        for step in range(2):
            push_d(2 * c + step, dz)
    pair_w.wait_recv()
    mine = pl.ds(y * 64, 64)
    copies_w = [push(wfull.at[mine], wfull.at[mine], sem_w.at[k], to) for k, to in enumerate(columns)]
    pair_d.wait_recv()
    for dz in range(1, NZ):
        for step in range(2):
            push_d(2 * other + step, dz)
    for dx in range(1, NX):
        push_d(lax.rem(x + dx, NX), 0)

    mine = pl.ds(rep * CH, CH)
    total = dbuf[mine, :].astype(F32)
    for dx, dz in REP_STEPS:
        slot = dx * NZ + dz
        remote(recv_d.at[slot], recv_d.at[slot], sem_d.at[slot], sibling).wait_recv()
        total = total + recv_d[slot].astype(F32)
    mean = total * (1.0 / NREP)
    for copy in copies_w:
        copy.wait_recv()
    parts = jnp.dot(jnp.concatenate(split3(mean), 0), wfull[...], preferred_element_type=F32)
    left = parts[0:CH] + parts[CH : 2 * CH] + parts[2 * CH :]

    for h in range(RANK // 128):
        product = outer_rows(left[:, 128 * h : 128 * h + 128], mean)
        for u in range(128 // UNIT):
            for r in range(NREP):
                i, j = UNIT * u + 8 * (r // 4), 128 * (r % 4)
                mpart[h * (128 // UNIT) + u, r] = product[i : i + 8, j : j + 128]
    lrow[...] = left
    leftbuf[mine, :] = left
    units = [pl.ds(start // UNIT, (stop - start) // UNIT) for start, stop in PIECES]
    copies_m = []
    for p, unit in enumerate(units):
        copies_m.append(
            [
                push(mpart.at[unit, chunk], recv_m.at[k, unit], sem_m.at[p, k], to)
                for k, (to, chunk) in enumerate(planes[p])
            ]
        )
    copies_lz = [push(lrow, leftbuf.at[mine], sem_lz.at[k], to) for k, to in enumerate(along_z)]

    copies_y, copies_f = [], []
    copies_lx = None
    for event in SCHEDULE:
        if event == "m":
            p = len(copies_y)
            for copy in copies_m[p]:
                copy.wait_recv()
            total = mpart[units[p], owned[p]]
            for k in range(len(replicas)):
                total = total + recv_m[k, units[p]]
            mrow[units[p]] = total
            copies_y.append(
                [push(mrow.at[units[p]], recv_y.at[k, units[p]], sem_y.at[p, k], to) for k, to in enumerate(lines[p])]
            )
        else:
            p = len(copies_f)
            for copy in copies_y[p]:
                copy.wait_recv()
            total = mrow[units[p]]
            for k in range(NY - 1):
                total = total + recv_y[k, units[p]]
            mfull[units[p], owned[p]] = total
            src = mfull.at[units[p], owned[p]]
            copies_f.append([push(src, src, sem_f.at[p, k], to) for k, (to, _) in enumerate(planes[p])])
            if p == 0:
                for copy in copies_lz:
                    copy.wait_recv()
                src = leftbuf.at[pl.ds(x * NZ * CH, NZ * CH)]
                copies_lx = [push(src, src, sem_lx.at[k], to) for k, to in enumerate(along_x)]
    waited = len(sends) - 2 * len(replicas)
    for copy in sends[:waited]:
        copy.wait_send()
    rank = jnp.where(c == 0, ranks_ref[0], ranks_ref[1])
    pairs = []
    for p, (start, stop) in enumerate(PIECES):
        n = stop - start
        block = start // 128 * 128
        less = None
        if p > 0:
            parts = [solved[i, 0:start, :] for i in range(3)]
            above = split3(a_ref[0:start, block : block + 128])
            above = jnp.concatenate([above[0], above[0], above[1], above[0], above[2], above[1]], 0)
            less = lax.dot_general(
                above, six_rows(parts), (((0,), (0,)), ((), ())), preferred_element_type=F32
            )[start - block : stop - block, :]
        for copy in copies_f[p]:
            copy.wait_recv()
        rows = []
        for u in range(start // UNIT, stop // UNIT):
            for g in range(8):
                rows.append(jnp.concatenate([mfull[u, 4 * g + t] for t in range(4)], 1))
        wide = jnp.concatenate(rows, 0)
        if p > 0:
            wide = wide - less[:, 0:COLS]
        parts = split3(wide)
        three = jnp.dot(jnp.concatenate(parts, 0), wfull[...], preferred_element_type=F32)
        row = lax.broadcasted_iota(jnp.int32, (n, RANK), 0)
        column = lax.broadcasted_iota(jnp.int32, (n, RANK), 1)
        filler = jnp.where((row + start == column) & (column >= rank), 1.0, 0.0)
        a_ref[start:stop, 0:RANK] = three[0:n] + three[n : 2 * n] + three[2 * n :] + filler
        a_ref[start:stop, RANK:] = jnp.where(row == column, 1.0, 0.0).astype(F32)[:, 0:128]
        eliminate_rows(a_ref, start, stop)
        inverse = six_lanes(a_ref[start:stop, RANK : RANK + n])
        mine = pl.ds(start, n)

        rows = jnp.dot(inverse, six_rows(parts), preferred_element_type=F32)
        last = stop == RANK
        factors_all[c, mine, :] = rows.astype(BF16)
        if not last:
            for i, part in enumerate(split3(rows)):
                solved[i, start:stop, 0:COLS] = part
        for t in range(4):
            blocks[t, mine, :] = rows[:, 128 * t : 128 * t + 128]
        src = factors_all.at[c, mine]
        pairs.append(push(src, src, sem_p.at[2 + 3 * p], sibling))
        pairs.append(push(blocks.at[y // 2, mine], piece_all.at[c, mine], sem_p.at[4 + 3 * p], sibling))
        piece_all[c, mine, :] = blocks[y // 2, mine, :]

        if p == 0:
            for copy in copies_lx:
                copy.wait_recv()
            for g in range(4):
                left_t[:, 128 * g : 128 * g + 128] = jnp.transpose(leftbuf[128 * g : 128 * g + 128, :])
        wide = left_t[start:stop, :]
        if p > 0:
            wide = wide - less[:, COLS:]
        rows = jnp.dot(inverse, six_rows(split3(wide)), preferred_element_type=F32)
        if not last:
            for i, part in enumerate(split3(rows)):
                solved[i, start:stop, COLS:] = part
        low_rows, high_rows = rows[:, 0:ROWS].astype(BF16), rows[:, ROWS:].astype(BF16)
        own_side = jnp.broadcast_to(c, (n, ROWS)) == 0
        obuf[mine, :] = jnp.where(own_side, high_rows, low_rows)
        pairs.append(push(obuf.at[mine], orth_all.at[c, mine], sem_p.at[3 + 3 * p], sibling))
        orth_all[c, mine, :] = jnp.where(own_side, low_rows, high_rows)
    for copy in pairs:
        copy.wait_recv()
    for copy in sends[waited:]:
        copy.wait_send()


def factor_all(ranks, deltas, warm):
    others, pieces = len(REP_STEPS), len(PIECES)
    total = 2 + others + (NY - 1) + pieces * (2 * others + NY - 1 + 3) + (NZ - 1) + (NX - 1)
    dma = pltpu.SemaphoreType.DMA
    return pl.pallas_call(
        factor_kernel,
        out_shape=(
            jax.ShapeDtypeStruct((2, RANK, ROWS), BF16),
            jax.ShapeDtypeStruct((2, RANK, COLS), BF16),
            jax.ShapeDtypeStruct((2, RANK, 128), F32),
        ),
        in_specs=[IN_HBM] * 3,
        out_specs=(VMEM,) * 3,
        scratch_shapes=[
            pltpu.SMEM((2,), jnp.int32),
            pltpu.VMEM((32, 2, RANK), F32),
            pltpu.VMEM((2 * ROWS, COLS), BF16),
            pltpu.VMEM((NREP, CH, COLS), BF16),
            pltpu.VMEM((2, 32, RANK), BF16),
            pltpu.VMEM((COLS, RANK), BF16),
            pltpu.VMEM((UNITS, NREP, 8, 128), F32),
            pltpu.VMEM((others, UNITS, 8, 128), F32),
            pltpu.VMEM((NY - 1, UNITS, 8, 128), F32),
            pltpu.VMEM((UNITS, 8, 128), F32),
            pltpu.VMEM((UNITS, NREP, 8, 128), F32),
            pltpu.VMEM((CH, RANK), F32),
            pltpu.VMEM((2 * ROWS, RANK), F32),
            pltpu.VMEM((RANK, 2 * ROWS), F32),
            pltpu.VMEM((RANK, RANK + 128), F32),
            pltpu.VMEM((3, RANK, WIDE), BF16),
            pltpu.VMEM((RANK, ROWS), BF16),
            pltpu.VMEM((4, RANK, 128), F32),
            dma((3,)), dma((total,)), dma((NREP,)), dma((pieces, others)), dma((pieces, NY - 1)),
            dma((pieces, others)), dma((NZ - 1,)), dma((NX - 1,)), dma((NY - 1,)), dma((2 + 3 * pieces,)),
        ],
        compiler_params=pltpu.CompilerParams(
            collective_id=1, has_side_effects=True, vmem_limit_bytes=32 * 2**20
        ),
        name="factor_all",
        cost_estimate=pl.CostEstimate(flops=10**9, bytes_accessed=0, transcendentals=0),
    )(*(pltpu.with_memory_space_constraint(a, pltpu.HBM) for a in (ranks, deltas, warm)))


def update_kernel(orth, factors, piece, weights, momentum, new_weights, new_momentum, new_factors, turned):
    offset = lax.axis_index("fsdp") % 4 * 32
    for m in range(2):
        approx = lax.dot_general(orth[m], factors[m], (((0,), (0,)), ((), ())), preferred_element_type=F32)
        fresh = OUTER_MOMENTUM * momentum[m] + approx
        new_momentum[m] = fresh
        new_weights[m] = weights[m] - OUTER_RATE * (approx + OUTER_MOMENTUM * fresh)
        turned[m] = jnp.transpose(piece[m])
        new_factors[:, m, :] = turned[m, pl.ds(offset, 32), :]


def update(orth, factors, piece, weights, momentum):
    return pl.pallas_call(
        update_kernel,
        out_shape=(
            jax.ShapeDtypeStruct((2, ROWS, COLS), F32),
            jax.ShapeDtypeStruct((2, ROWS, COLS), F32),
            jax.ShapeDtypeStruct((32, 2, RANK), F32),
        ),
        in_specs=[VMEM] * 5,
        out_specs=(VMEM,) * 3,
        scratch_shapes=[pltpu.VMEM((2, 128, RANK), F32)],
        compiler_params=pltpu.CompilerParams(vmem_limit_bytes=32 * 2**20),
        name="update",
    )(orth, factors, piece, weights, momentum)


def shards(deltas, weights, momentum, warm_factors, matrix_ranks):
    orth, factors, piece = factor_all(matrix_ranks, deltas, warm_factors)
    return update(orth, factors, piece, weights, momentum)


def solution(mesh):
    placed = (
        P("rep", None, "fsdp", None),
        P(None, "fsdp", None),
        P(None, "fsdp", None),
        P("fsdp", None, None),
        P(),
    )
    return jax.shard_map(
        shards,
        mesh=mesh,
        in_specs=placed,
        out_specs=(P(None, "fsdp", None), P(None, "fsdp", None), P("fsdp", None, None)),
        check_vma=False,
    )
```

time: 72.9 us -> 70 us (0.960)
  Pallas kernels: 72.1 us -> 69.2 us
    pallas_call x1, Pallas kernels: 70.3 us -> 67.4 us  [factor_all(): pl.pallas_call(factor_kernel, out_shape=(jax.ShapeDtypeStruct((2, RANK, R...]
where the time goes in v3:
time: 70 us; the launch traced here: 69.9 us
  Pallas kernels  69.2 us (99%)
    pallas_call x1, Pallas kernels, factor_all(): pl.pallas_call(factor_kernel, out_shape=(jax.ShapeDtypeStruct((2, RANK, R...  67.4 us
    pallas_call x1, Pallas kernels, update(): pl.pallas_call(update_kernel, out_shape=(jax.ShapeDtypeStruct((2, ROWS, C...  1.78 us

profile of v3, /device:TPU:1, one launch (start us, length us, event | category | flops | bytes accessed | tf_op | source)
XLA Modules:
  0.0 69.9 jit_solution(3752956202701300788)
XLA Ops:
  0.6 0.0 copy-start.1
  0.6 0.0 copy-start
  0.7 67.4 %factor_all.1 = (bf16[2,256,256]{2,1,0:T(8,128)(2,1)S(1)}, bf16[2,256,512]{2,1,0:T(8,128)(2,1)S(1)}, f32[2,256,128]{2,1,0:T(8,128)S(1)}) custom-call(s32[2]{0:T(128)} %ranks_hbm.1, bf16[1,2,256,512]{3,2,1,0:T(8,128)(2,1)} %deltas_hbm.1, f32[32,2,256]{2,1,0:T(2,128)} %warm_hbm.1), custom_call_target="tpu_custom_call" | custom-call | flops 1000000000 | tf_op jit(solution)/shard_map/factor_all/pallas_call | solution.py:337
  68.1 0.0 copy-done.1
  68.1 0.0 copy-done
  68.1 1.8 %update.1 = (f32[2,256,512]{2,1,0:T(8,128)}, f32[2,256,512]{2,1,0:T(8,128)}, f32[32,2,256]{2,1,0:T(2,128)}) custom-call(bf16[2,256,256]{2,1,0:T(8,128)(2,1)S(1)} %get-tuple-element.6.orth, bf16[2,256,512]{2,1,0:T(8,128)(2,1)S(1)} %get-tuple-element.7.factors, f32[2,256,128]{2,1,0:T(8,128)S(1)} %get-tuple-element.8.piece, f32[2,256,512]{2,1,0:T(8,128)S(1)} %copy-done, ...), custom_call_target="tpu_custom_call" | custom-call | tf_op jit(solution)/shard_map/update/pallas_call | solution.py:388
Async XLA Ops:
  0.6 67.5 %copy-start.1 = (f32[2,256,512]{2,1,0:T(8,128)S(1)}, f32[2,256,512]{2,1,0:T(8,128)}, u32[]{:S(2)}) copy-start(f32[2,256,512]{2,1,0:T(8,128)} %momentum.1) | copy-start | bytes 3145732
  0.6 67.5 %copy-start = (f32[2,256,512]{2,1,0:T(8,128)S(1)}, f32[2,256,512]{2,1,0:T(8,128)}, u32[]{:S(2)}) copy-start(f32[2,256,512]{2,1,0:T(8,128)} %weights.1) | copy-start | bytes 3145732

commit v4 on v3

--- a/solution.py
+++ b/solution.py
@@ -18,7 +18,7 @@
 UNITS = RANK // UNIT
 PIECES = ((0, 128), (128, 256))
 PLANES = "zy"
-SCHEDULE = "mmyy"
+SCHEDULE = "mmlyy"
 WIDE = COLS + 2 * ROWS
 VMEM = pl.BlockSpec(memory_space=pltpu.VMEM)
 IN_HBM = pl.BlockSpec(memory_space=pltpu.HBM)
@@ -243,6 +243,11 @@
             copies_y.append(
                 [push(mrow.at[units[p]], recv_y.at[k, units[p]], sem_y.at[p, k], to) for k, to in enumerate(lines[p])]
             )
+        elif event == "l":
+            for copy in copies_lz:
+                copy.wait_recv()
+            src = leftbuf.at[pl.ds(x * NZ * CH, NZ * CH)]
+            copies_lx = [push(src, src, sem_lx.at[k], to) for k, to in enumerate(along_x)]
         else:
             p = len(copies_f)
             for copy in copies_y[p]:
@@ -253,14 +258,14 @@
             mfull[units[p], owned[p]] = total
             src = mfull.at[units[p], owned[p]]
             copies_f.append([push(src, src, sem_f.at[p, k], to) for k, (to, _) in enumerate(planes[p])])
-            if p == 0:
-                for copy in copies_lz:
-                    copy.wait_recv()
-                src = leftbuf.at[pl.ds(x * NZ * CH, NZ * CH)]
-                copies_lx = [push(src, src, sem_lx.at[k], to) for k, to in enumerate(along_x)]
     waited = len(sends) - 2 * len(replicas)
     for copy in sends[:waited]:
         copy.wait_send()
+    for copy in copies_lx:
+        copy.wait_recv()
+    for g in range(4):
+        left_t[:, 128 * g : 128 * g + 128] = jnp.transpose(leftbuf[128 * g : 128 * g + 128, :])
+
     rank = jnp.where(c == 0, ranks_ref[0], ranks_ref[1])
     pairs = []
     for p, (start, stop) in enumerate(PIECES):
@@ -307,11 +312,6 @@
         pairs.append(push(blocks.at[y // 2, mine], piece_all.at[c, mine], sem_p.at[4 + 3 * p], sibling))
         piece_all[c, mine, :] = blocks[y // 2, mine, :]
 
-        if p == 0:
-            for copy in copies_lx:
-                copy.wait_recv()
-            for g in range(4):
-                left_t[:, 128 * g : 128 * g + 128] = jnp.transpose(leftbuf[128 * g : 128 * g + 128, :])
         wide = left_t[start:stop, :]
         if p > 0:
             wide = wide - less[:, COLS:]

time: 70 us -> 68.7 us (0.981)
  Pallas kernels: 69.2 us -> 67.9 us
    pallas_call x1, Pallas kernels: 67.4 us -> 66.1 us  [factor_all(): pl.pallas_call(factor_kernel, out_shape=(jax.ShapeDtypeStruct((2, RANK, R...]
where the time goes in v4:
time: 68.7 us; the launch traced here: 68.5 us
  Pallas kernels  67.9 us (99%)
    pallas_call x1, Pallas kernels, factor_all(): pl.pallas_call(factor_kernel, out_shape=(jax.ShapeDtypeStruct((2, RANK, R...  66.1 us
    pallas_call x1, Pallas kernels, update(): pl.pallas_call(update_kernel, out_shape=(jax.ShapeDtypeStruct((2, ROWS, C...  1.78 us

profile of v4, /device:TPU:1, one launch (start us, length us, event | category | flops | bytes accessed | tf_op | source)
XLA Modules:
  0.0 68.5 jit_solution(3360309863299533299)
XLA Ops:
  0.6 0.0 copy-start.1
  0.6 0.0 copy-start
  0.7 66.1 %factor_all.1 = (bf16[2,256,256]{2,1,0:T(8,128)(2,1)S(1)}, bf16[2,256,512]{2,1,0:T(8,128)(2,1)S(1)}, f32[2,256,128]{2,1,0:T(8,128)S(1)}) custom-call(s32[2]{0:T(128)} %ranks_hbm.1, bf16[1,2,256,512]{3,2,1,0:T(8,128)(2,1)} %deltas_hbm.1, f32[32,2,256]{2,1,0:T(2,128)} %warm_hbm.1), custom_call_target="tpu_custom_call" | custom-call | flops 1000000000 | tf_op jit(solution)/shard_map/factor_all/pallas_call | solution.py:337
  66.7 0.0 copy-done.1
  66.7 0.0 copy-done
  66.8 1.8 %update.1 = (f32[2,256,512]{2,1,0:T(8,128)}, f32[2,256,512]{2,1,0:T(8,128)}, f32[32,2,256]{2,1,0:T(2,128)}) custom-call(bf16[2,256,256]{2,1,0:T(8,128)(2,1)S(1)} %get-tuple-element.6.orth, bf16[2,256,512]{2,1,0:T(8,128)(2,1)S(1)} %get-tuple-element.7.factors, f32[2,256,128]{2,1,0:T(8,128)S(1)} %get-tuple-element.8.piece, f32[2,256,512]{2,1,0:T(8,128)S(1)} %copy-done, ...), custom_call_target="tpu_custom_call" | custom-call | tf_op jit(solution)/shard_map/update/pallas_call | solution.py:388
Async XLA Ops:
  0.6 66.1 %copy-start.1 = (f32[2,256,512]{2,1,0:T(8,128)S(1)}, f32[2,256,512]{2,1,0:T(8,128)}, u32[]{:S(2)}) copy-start(f32[2,256,512]{2,1,0:T(8,128)} %momentum.1) | copy-start | bytes 3145732
  0.6 66.1 %copy-start = (f32[2,256,512]{2,1,0:T(8,128)S(1)}, f32[2,256,512]{2,1,0:T(8,128)}, u32[]{:S(2)}) copy-start(f32[2,256,512]{2,1,0:T(8,128)} %weights.1) | copy-start | bytes 3145732

commit v5 on v4

--- a/solution.py
+++ b/solution.py
@@ -279,6 +279,10 @@
             less = lax.dot_general(
                 above, six_rows(parts), (((0,), (0,)), ((), ())), preferred_element_type=F32
             )[start - block : stop - block, :]
+        left_rows = left_t[start:stop, :]
+        if p > 0:
+            left_rows = left_rows - less[:, COLS:]
+        left_rows = six_rows(split3(left_rows))
         for copy in copies_f[p]:
             copy.wait_recv()
         rows = []
@@ -312,10 +316,7 @@
         pairs.append(push(blocks.at[y // 2, mine], piece_all.at[c, mine], sem_p.at[4 + 3 * p], sibling))
         piece_all[c, mine, :] = blocks[y // 2, mine, :]
 
-        wide = left_t[start:stop, :]
-        if p > 0:
-            wide = wide - less[:, COLS:]
-        rows = jnp.dot(inverse, six_rows(split3(wide)), preferred_element_type=F32)
+        rows = jnp.dot(inverse, left_rows, preferred_element_type=F32)
         if not last:
             for i, part in enumerate(split3(rows)):
                 solved[i, start:stop, COLS:] = part

time: 68.7 us -> 68.7 us (level)
  no operation moved by 1% of the time
where the time goes in v5:
time: 68.7 us; the launch traced here: 68.6 us
  Pallas kernels  67.9 us (99%)
    pallas_call x1, Pallas kernels, factor_all(): pl.pallas_call(factor_kernel, out_shape=(jax.ShapeDtypeStruct((2, RANK, R...  66.1 us
    pallas_call x1, Pallas kernels, update(): pl.pallas_call(update_kernel, out_shape=(jax.ShapeDtypeStruct((2, ROWS, C...  1.78 us

profile of v5, /device:TPU:1, one launch (start us, length us, event | category | flops | bytes accessed | tf_op | source)
XLA Modules:
  0.0 68.6 jit_solution(12125197410403962722)
XLA Ops:
  0.6 0.0 copy-start.1
  0.6 0.0 copy-start
  0.7 66.1 %factor_all.1 = (bf16[2,256,256]{2,1,0:T(8,128)(2,1)S(1)}, bf16[2,256,512]{2,1,0:T(8,128)(2,1)S(1)}, f32[2,256,128]{2,1,0:T(8,128)S(1)}) custom-call(s32[2]{0:T(128)} %ranks_hbm.1, bf16[1,2,256,512]{3,2,1,0:T(8,128)(2,1)} %deltas_hbm.1, f32[32,2,256]{2,1,0:T(2,128)} %warm_hbm.1), custom_call_target="tpu_custom_call" | custom-call | flops 1000000000 | tf_op jit(solution)/shard_map/factor_all/pallas_call | solution.py:338
  66.8 0.0 copy-done.1
  66.8 0.0 copy-done
  66.8 1.8 %update.1 = (f32[2,256,512]{2,1,0:T(8,128)}, f32[2,256,512]{2,1,0:T(8,128)}, f32[32,2,256]{2,1,0:T(2,128)}) custom-call(bf16[2,256,256]{2,1,0:T(8,128)(2,1)S(1)} %get-tuple-element.6.orth, bf16[2,256,512]{2,1,0:T(8,128)(2,1)S(1)} %get-tuple-element.7.factors, f32[2,256,128]{2,1,0:T(8,128)S(1)} %get-tuple-element.8.piece, f32[2,256,512]{2,1,0:T(8,128)S(1)} %copy-done, ...), custom_call_target="tpu_custom_call" | custom-call | tf_op jit(solution)/shard_map/update/pallas_call | solution.py:389
Async XLA Ops:
  0.6 66.1 %copy-start.1 = (f32[2,256,512]{2,1,0:T(8,128)S(1)}, f32[2,256,512]{2,1,0:T(8,128)}, u32[]{:S(2)}) copy-start(f32[2,256,512]{2,1,0:T(8,128)} %momentum.1) | copy-start | bytes 3145732
  0.6 66.1 %copy-start = (f32[2,256,512]{2,1,0:T(8,128)S(1)}, f32[2,256,512]{2,1,0:T(8,128)}, u32[]{:S(2)}) copy-start(f32[2,256,512]{2,1,0:T(8,128)} %weights.1) | copy-start | bytes 3145732
